TPU v7x, 32 devices: a whole 2x2x4 slice. The times are simulated.
32 devices in a mesh: comm: 8 (over z, x), sub: 4 (over y, core).
Axes of the slice: x: 2, y: 2, z: 4, core: 2. Of those that a mesh axis runs over, the one named last changes fastest.
Arguments:
- features: float32 [73728, 1024], P(('comm', 'sub')), may hold values from -6 to 6
- q_weight: float32 [1024, 1024], P(('comm', 'sub')), may hold values from -0.1875 to 0.1875
- q_bias: float32 [1024], P(('comm', 'sub')), may hold values from -3 to 3
- w_weight: float32 [2048, 1024], P(('comm', 'sub')), may hold values from -0.125 to 0.125
- w_bias: float32 [1024], P(('comm', 'sub')), may hold values from -3 to 3
- nbr_index: int32 [73728, 50], P(('comm', 'sub')), may hold values from 0 to 2431
- nbr_count: int32 [73728], P(('comm', 'sub')), may hold values from 5 to 50
- importance: float32 [73728, 50], P(('comm', 'sub')), may hold values from 0.1 to 10
- send_rows: int32 [32, 32, 4], P(('comm', 'sub')), may hold values from 0 to 2303
- cotangent: float32 [73728, 1024], P(('comm', 'sub')), may hold values from -6 to 6
Outputs:
- embedding: float32 [73728, 1024], P(('comm', 'sub'))
- grad_features: float32 [73728, 1024], P(('comm', 'sub'))
- grad_q_weight: float32 [1024, 1024], P(('comm', 'sub'))
- grad_q_bias: float32 [1024], P(('comm', 'sub'))
- grad_w_weight: float32 [2048, 1024], P(('comm', 'sub'))
- grad_w_bias: float32 [1024], P(('comm', 'sub'))
All inputs are finite; a program needn't handle non-finite values.
Results may differ from a plain program's by a relative error of at most 0.0085.
Values may be sent and summed in bfloat16 or wider, within the bound.
A program may use at most 256 MiB of HBM per device.

v0:
```python
import math

import jax
import jax.numpy as jnp
from jax import lax
from jax.sharding import PartitionSpec as P


def finish(pre_out):
    act = jax.nn.gelu(pre_out)
    return act * lax.rsqrt(jnp.mean(act * act, axis=1, keepdims=True) + 1e-06)


def blend_parts(index_block, alpha_block, table_rows):
    columns = lax.broadcasted_iota(jnp.int32, (1, 1, table_rows), 2)
    hits = index_block[:, :, None] == columns
    mixing = jnp.sum(jnp.where(hits, alpha_block.astype(jnp.float32)[:, :, None], 0.0), axis=1)
    upper = mixing.astype(jnp.bfloat16)
    lower = (mixing - upper.astype(jnp.float32)).astype(jnp.bfloat16)
    return (upper, lower)


def shards(
    features,
    q_weight,
    q_bias,
    w_weight,
    w_bias,
    nbr_index,
    nbr_count,
    importance,
    send_rows,
    cotangent,
):
    devices = lax.axis_size(("comm", "sub"))
    rows, width = features.shape
    fanout = nbr_index.shape[1]
    per_peer = send_rows.shape[2]
    table_rows = rows + devices * per_peer
    block = math.gcd(rows, 256)
    steps_count = rows // block
    q_full, w_full, qbias_full, wbias_full = (
        lax.all_gather(q_weight.astype(jnp.bfloat16), ("comm", "sub"), axis=0, tiled=True),
        lax.all_gather(w_weight.astype(jnp.bfloat16), ("comm", "sub"), axis=0, tiled=True),
        lax.all_gather(q_bias.astype(jnp.bfloat16), ("comm", "sub"), axis=0, tiled=True),
        lax.all_gather(w_bias.astype(jnp.bfloat16), ("comm", "sub"), axis=0, tiled=True),
    )
    feat_low = features.astype(jnp.bfloat16)
    pre_hidden = jnp.dot(feat_low, q_full, preferred_element_type=jnp.float32) + qbias_full.astype(
        jnp.float32
    )
    neigh_low = jax.nn.gelu(pre_hidden).astype(jnp.bfloat16)
    targets = send_rows[0]
    outgoing = neigh_low[targets]
    incoming = lax.all_to_all(outgoing, ("comm", "sub"), split_axis=0, concat_axis=0, tiled=True)
    table = jnp.concatenate([neigh_low, incoming.reshape(devices * per_peer, width)], axis=0)
    present = lax.broadcasted_iota(jnp.int32, (rows, fanout), 1) < nbr_count[:, None]
    weights = jnp.where(present, importance, jnp.zeros_like(importance))
    alpha = (weights / jnp.sum(weights, axis=1, keepdims=True)).astype(jnp.bfloat16)
    index_blocks = nbr_index.reshape(steps_count, block, fanout)
    alpha_blocks = alpha.reshape(steps_count, block, fanout)

    def pool_step(pair):
        upper, lower = blend_parts(pair[0], pair[1], table_rows)
        return jnp.dot(upper, table, preferred_element_type=jnp.float32) + jnp.dot(
            lower, table, preferred_element_type=jnp.float32
        )

    pooled = lax.map(pool_step, (index_blocks, alpha_blocks)).reshape(rows, width)
    joined = jnp.concatenate([feat_low, pooled.astype(jnp.bfloat16)], axis=1)
    pre_out = jnp.dot(joined, w_full, preferred_element_type=jnp.float32) + wbias_full.astype(
        jnp.float32
    )
    embedding, finish_back = jax.vjp(finish, pre_out)
    grad_pre_out = finish_back(cotangent)[0].astype(jnp.bfloat16)
    grad_w = lax.dot_general(
        joined, grad_pre_out, (((0,), (0,)), ((), ())), preferred_element_type=jnp.float32
    )
    grad_wbias = jnp.sum(grad_pre_out.astype(jnp.float32), axis=0)
    grad_joined = lax.dot_general(
        grad_pre_out, w_full, (((1,), (1,)), ((), ())), preferred_element_type=jnp.float32
    )
    grad_pooled = grad_joined[:, width:]
    contract = (((0,), (0,)), ((), ()))

    def spread(step, accum):
        index_block = lax.dynamic_slice_in_dim(nbr_index, step * block, block, 0)
        alpha_block = lax.dynamic_slice_in_dim(alpha, step * block, block, 0)
        grad_block = lax.dynamic_slice_in_dim(grad_pooled, step * block, block, 0)
        upper, lower = blend_parts(index_block, alpha_block, table_rows)
        grad_upper = grad_block.astype(jnp.bfloat16)
        grad_lower = (grad_block - grad_upper.astype(jnp.float32)).astype(jnp.bfloat16)
        accum = accum + lax.dot_general(
            upper, grad_upper, contract, preferred_element_type=jnp.float32
        )
        accum = accum + lax.dot_general(
            upper, grad_lower, contract, preferred_element_type=jnp.float32
        )
        return accum + lax.dot_general(
            lower, grad_upper, contract, preferred_element_type=jnp.float32
        )

    grad_table = lax.fori_loop(0, steps_count, spread, jnp.zeros((table_rows, width), jnp.float32))
    outgoing_grad = grad_table[rows:].reshape(devices, per_peer, width)
    returned = lax.all_to_all(
        outgoing_grad, ("comm", "sub"), split_axis=0, concat_axis=0, tiled=True
    )
    grad_neigh = (
        grad_table[:rows].at[targets.reshape(-1)].add(returned.reshape(devices * per_peer, width))
    )
    gelu_value, gelu_back = jax.vjp(jax.nn.gelu, pre_hidden)
    grad_pre_hidden = gelu_back(grad_neigh)[0].astype(jnp.bfloat16)
    grad_q = lax.dot_general(
        feat_low, grad_pre_hidden, (((0,), (0,)), ((), ())), preferred_element_type=jnp.float32
    )
    grad_qbias = jnp.sum(grad_pre_hidden.astype(jnp.float32), axis=0)
    grad_features = grad_joined[:, :width] + lax.dot_general(
        grad_pre_hidden, q_full, (((1,), (1,)), ((), ())), preferred_element_type=jnp.float32
    )
    grad_q_shard, grad_w_shard, grad_qbias_shard, grad_wbias_shard = (
        lax.psum_scatter(grad_q, ("comm", "sub"), scatter_dimension=0, tiled=True),
        lax.psum_scatter(grad_w, ("comm", "sub"), scatter_dimension=0, tiled=True),
        lax.psum_scatter(grad_qbias, ("comm", "sub"), scatter_dimension=0, tiled=True),
        lax.psum_scatter(grad_wbias, ("comm", "sub"), scatter_dimension=0, tiled=True),
    )
    return (
        embedding,
        grad_features,
        grad_q_shard,
        grad_qbias_shard,
        grad_w_shard,
        grad_wbias_shard,
    )


def solution(mesh):
    in_specs = (
        P(("comm", "sub"), None),
        P(("comm", "sub"), None),
        P(("comm", "sub")),
        P(("comm", "sub"), None),
        P(("comm", "sub")),
        P(("comm", "sub"), None),
        P(("comm", "sub")),
        P(("comm", "sub"), None),
        P(("comm", "sub"), None, None),
        P(("comm", "sub"), None),
    )
    out_specs = (
        P(("comm", "sub"), None),
        P(("comm", "sub"), None),
        P(("comm", "sub"), None),
        P(("comm", "sub")),
        P(("comm", "sub"), None),
        P(("comm", "sub")),
    )
    return jax.shard_map(shards, mesh=mesh, in_specs=in_specs, out_specs=out_specs, check_vma=False)
```

profile of v0, /device:TPU:0, one launch (start us, length us, event | category | flops | bytes accessed | tf_op | source)
XLA Modules:
  0.0 1200.4 jit_solution(4618446470939030442)
XLA Ops:
  13.0 42.0 %all-reduce.5 = (bf16[1024]{0:T(1024)(128)(2,1)S(1)}, bf16[1024]{0:T(1024)(128)(2,1)S(1)}) all-reduce(bf16[1024]{0:T(1024)(128)(2,1)S(1)} %dynamic-update-slice, bf16[1024]{0:T(1024)(128)(2,1)S(1)} %dynamic-update-slice.1), channel_id=1, replica_groups=mesh['comm'=8,'sub'=4] {'comm','sub'}, use_global_device_ids=true, to_apply=%add | all-reduce | flops 2048 | bytes 8192
  61.9 8.8 all-gather.3.cloned.1.call-done
  70.7 13.4 %multiply_convert_fusion = (bf16[2304,1024]{1,0:T(8,128)(2,1)}, f32[2304,1024]{1,0:T(8,128)}) fusion(f32[1024]{0:T(1024)S(1)} %convert_element_type.117, bf16[2304,1024]{1,0:T(8,128)(2,1)} %convert_element_type.113, bf16[1024,1024]{1,0:T(8,128)(2,1)} %all-gather.3.cloned.1.call-done), kind=kOutput, calls=%fused_computation.55 | convolution fusion | flops 4855431168 | bytes 20975616 | tf_op jit(solution)/shard_map/dot_general | solution.py:49
  92.9 10.3 all-to-all-done
  108.5 240.3 %while.24 = (s32[]{:T(128)}, bf16[9,256,1024]{2,1,0:T(8,128)(2,1)}, s32[9,256,50]{1,0,2:T(8,128)S(1)}, bf16[9,256,50]{1,2,0:T(8,128)(2,1)S(1)}, bf16[2432,1024]{1,0:T(8,128)(2,1)}, /*index=5*/s32[]{:T(128)}) while((s32[]{:T(128)}, bf16[9,256,1024]{2,1,0:T(8,128)(2,1)}, s32[9,256,50]{1,0,2:T(8,128)S(1)}, bf16[9,256,50]{1,2,0:T(8,128)(2,1)S(1)}, ...), condition=%wide.region_3.4_spmd, body=%wide.region_1.3_spmd.sunk | while | flops 2646290944 | bytes 35904648 | solution.py:69
  108.5 20.1 %select_reduce_fusion.4 = f32[256,2432]{1,0:T(8,128)S(1)} fusion(f32[256,50]{0,1:T(8,128)S(1)} %bitcast_convert_fusion.2, s32[256,50]{0,1:T(8,128)S(1)} %bitcast.46), kind=kLoop, calls=%fused_computation.2.clone.1 | loop fusion | flops 92766208 | bytes 2592768 | tf_op jit(solution)/shard_map/while/body/eval_jaxpr/reduce_sum | solution.py:17
  135.3 20.1 %select_reduce_fusion.4 = f32[256,2432]{1,0:T(8,128)S(1)} fusion(f32[256,50]{0,1:T(8,128)S(1)} %bitcast_convert_fusion.2, s32[256,50]{0,1:T(8,128)S(1)} %bitcast.46), kind=kLoop, calls=%fused_computation.2.clone.1 | loop fusion | flops 92766208 | bytes 2592768 | tf_op jit(solution)/shard_map/while/body/eval_jaxpr/reduce_sum | solution.py:17
  162.0 20.1 %select_reduce_fusion.4 = f32[256,2432]{1,0:T(8,128)S(1)} fusion(f32[256,50]{0,1:T(8,128)S(1)} %bitcast_convert_fusion.2, s32[256,50]{0,1:T(8,128)S(1)} %bitcast.46), kind=kLoop, calls=%fused_computation.2.clone.1 | loop fusion | flops 92766208 | bytes 2592768 | tf_op jit(solution)/shard_map/while/body/eval_jaxpr/reduce_sum | solution.py:17
  188.7 20.1 %select_reduce_fusion.4 = f32[256,2432]{1,0:T(8,128)S(1)} fusion(f32[256,50]{0,1:T(8,128)S(1)} %bitcast_convert_fusion.2, s32[256,50]{0,1:T(8,128)S(1)} %bitcast.46), kind=kLoop, calls=%fused_computation.2.clone.1 | loop fusion | flops 92766208 | bytes 2592768 | tf_op jit(solution)/shard_map/while/body/eval_jaxpr/reduce_sum | solution.py:17
  215.4 20.1 %select_reduce_fusion.4 = f32[256,2432]{1,0:T(8,128)S(1)} fusion(f32[256,50]{0,1:T(8,128)S(1)} %bitcast_convert_fusion.2, s32[256,50]{0,1:T(8,128)S(1)} %bitcast.46), kind=kLoop, calls=%fused_computation.2.clone.1 | loop fusion | flops 92766208 | bytes 2592768 | tf_op jit(solution)/shard_map/while/body/eval_jaxpr/reduce_sum | solution.py:17
  242.1 20.1 %select_reduce_fusion.4 = f32[256,2432]{1,0:T(8,128)S(1)} fusion(f32[256,50]{0,1:T(8,128)S(1)} %bitcast_convert_fusion.2, s32[256,50]{0,1:T(8,128)S(1)} %bitcast.46), kind=kLoop, calls=%fused_computation.2.clone.1 | loop fusion | flops 92766208 | bytes 2592768 | tf_op jit(solution)/shard_map/while/body/eval_jaxpr/reduce_sum | solution.py:17
  268.7 20.1 %select_reduce_fusion.4 = f32[256,2432]{1,0:T(8,128)S(1)} fusion(f32[256,50]{0,1:T(8,128)S(1)} %bitcast_convert_fusion.2, s32[256,50]{0,1:T(8,128)S(1)} %bitcast.46), kind=kLoop, calls=%fused_computation.2.clone.1 | loop fusion | flops 92766208 | bytes 2592768 | tf_op jit(solution)/shard_map/while/body/eval_jaxpr/reduce_sum | solution.py:17
  295.4 20.1 %select_reduce_fusion.4 = f32[256,2432]{1,0:T(8,128)S(1)} fusion(f32[256,50]{0,1:T(8,128)S(1)} %bitcast_convert_fusion.2, s32[256,50]{0,1:T(8,128)S(1)} %bitcast.46), kind=kLoop, calls=%fused_computation.2.clone.1 | loop fusion | flops 92766208 | bytes 2592768 | tf_op jit(solution)/shard_map/while/body/eval_jaxpr/reduce_sum | solution.py:17
  322.1 20.1 %select_reduce_fusion.4 = f32[256,2432]{1,0:T(8,128)S(1)} fusion(f32[256,50]{0,1:T(8,128)S(1)} %bitcast_convert_fusion.2, s32[256,50]{0,1:T(8,128)S(1)} %bitcast.46), kind=kLoop, calls=%fused_computation.2.clone.1 | loop fusion | flops 92766208 | bytes 2592768 | tf_op jit(solution)/shard_map/while/body/eval_jaxpr/reduce_sum | solution.py:17
  348.7 17.7 %multiply_reduce_fusion = (f32[2304]{0:T(1024)S(1)}, f32[2304]{0:T(1024)S(1)}, f32[2304,1024]{1,0:T(8,128)S(1)}) fusion(f32[2304,1024]{1,0:T(8,128)} %param.23, f32[1024]{0:T(1024)S(1)} %convert_element_type.123, bf16[2048,1024]{1,0:T(8,128)(2,1)} %all-gather.5.cloned.1.call-done, bf16[2304,1024]{1,0:T(8,128)(2,1)} %bitcast.51, ...), kind=kOutput, calls=%fused_computation.53 | convolution fusion | flops 9713217536 | bytes 32528384 | tf_op jit(solution)/shard_map/dot_general | solution.py:71
  366.4 13.9 %convert_reduce_fusion = (f32[1024]{0:T(1024)}, bf16[2304,1024]{1,0:T(8,128)(2,1)S(1)}, f32[2304,1024]{1,0:T(8,128)}) fusion(f32[2304]{0:T(1024)S(1)} %get-tuple-element.218, f32[2304,1024]{1,0:T(8,128)S(1)} %get-tuple-element.222, f32[1024]{0:T(1024)S(1)} %convert_element_type.123, f32[2304,1024]{1,0:T(8,128)} %param.23, f32[2304]{0:T(1024)S(1)} %get-tuple-element.219), kind=kLoop, calls=%fused_computation.51 | loop fusion | flops 68418560 | bytes 33056768 | tf_op jit(solution)/shard_map/reduce_sum | solution.py:79
  382.5 12.5 %fusion.37 = f32[2304,2048]{1,0:T(8,128)S(1)} fusion(bf16[2304,1024]{1,0:T(8,128)(2,1)S(1)} %get-tuple-element.214, bf16[2048,1024]{1,0:T(8,128)(2,1)} %all-gather.5.cloned.1.call-done), kind=kOutput, calls=%fused_computation.75 | convolution fusion | flops 9663676416 | bytes 27787264 | tf_op jit(solution)/shard_map/dot_general | solution.py:80
  404.3 446.7 %while.25 = (s32[]{:T(128)}, f32[2432,1024]{1,0:T(8,128)}, s32[2304,50]{0,1:T(8,128)}, bf16[2304,50]{0,1:T(8,128)(2,1)S(1)}, f32[2304,1024]{1,0:T(8,128)}, /*index=5*/s32[]{:T(128)}, s32[]{:T(128)}, s32[]{:T(128)}, s32[]{:T(128)}) while((s32[]{:T(128)}, f32[2432,1024]{1,0:T(8,128)}, s32[2304,50]{0,1:T(8,128)}, ...), condition=%wide.region_8.9_spmd.clone, body=%wide.region_6.8_spmd.clone.sunk | while | flops 3932467712 | bytes 72633520 | solution.py:103
  405.1 20.1 %select_reduce_fusion.5 = f32[256,2432]{1,0:T(8,128)S(1)} fusion(f32[256,50]{0,1:T(8,128)S(1)} %dynamic-slice_convert_fusion.10, s32[256,50]{0,1:T(8,128)S(1)} %constant_dynamic-slice_fusion.5), kind=kLoop, calls=%fused_computation.14.clone.1 | loop fusion | flops 92766208 | bytes 2592768 | tf_op jit(solution)/shard_map/while/body/eval_jaxpr/reduce_sum | solution.py:17
  438.7 12.7 %fusion.69 = f32[2432,1024]{1,0:T(8,128)} fusion(f32[2432,1024]{1,0:T(8,128)} %fusion.67, f32[2432,1024]{1,0:T(8,128)} %fusion.68, f32[2432,1024]{1,0:T(8,128)} %get-tuple-element.313, pred[]{:T(512)S(6)} %compare.3, f32[256,2432]{1,0:T(8,128)S(1)} %select_reduce_fusion.5, f32[2304,1024]{1,0:T(8,128)} %get-tuple-element.325, s32[]{:T(128)S(6)} %select_n.65), kind=kOutput, calls=%fused_computation.18.clone.1 | convolution fusion | flops 1287520256 | bytes 42860548 | tf_op jit(solution)/shard_map/while/body/eval_jaxpr/dot_general | solution.py:99
  452.2 20.1 %select_reduce_fusion.5 = f32[256,2432]{1,0:T(8,128)S(1)} fusion(f32[256,50]{0,1:T(8,128)S(1)} %dynamic-slice_convert_fusion.10, s32[256,50]{0,1:T(8,128)S(1)} %constant_dynamic-slice_fusion.5), kind=kLoop, calls=%fused_computation.14.clone.1 | loop fusion | flops 92766208 | bytes 2592768 | tf_op jit(solution)/shard_map/while/body/eval_jaxpr/reduce_sum | solution.py:17
  478.9 7.0 fusion.67
  485.9 15.5 %fusion.69 = f32[2432,1024]{1,0:T(8,128)} fusion(f32[2432,1024]{1,0:T(8,128)} %fusion.67, f32[2432,1024]{1,0:T(8,128)} %fusion.68, f32[2432,1024]{1,0:T(8,128)} %get-tuple-element.313, pred[]{:T(512)S(6)} %compare.3, f32[256,2432]{1,0:T(8,128)S(1)} %select_reduce_fusion.5, f32[2304,1024]{1,0:T(8,128)} %get-tuple-element.325, s32[]{:T(128)S(6)} %select_n.65), kind=kOutput, calls=%fused_computation.18.clone.1 | convolution fusion | flops 1287520256 | bytes 42860548 | tf_op jit(solution)/shard_map/while/body/eval_jaxpr/dot_general | solution.py:99
  502.2 20.1 %select_reduce_fusion.5 = f32[256,2432]{1,0:T(8,128)S(1)} fusion(f32[256,50]{0,1:T(8,128)S(1)} %dynamic-slice_convert_fusion.10, s32[256,50]{0,1:T(8,128)S(1)} %constant_dynamic-slice_fusion.5), kind=kLoop, calls=%fused_computation.14.clone.1 | loop fusion | flops 92766208 | bytes 2592768 | tf_op jit(solution)/shard_map/while/body/eval_jaxpr/reduce_sum | solution.py:17
  535.8 15.5 %fusion.69 = f32[2432,1024]{1,0:T(8,128)} fusion(f32[2432,1024]{1,0:T(8,128)} %fusion.67, f32[2432,1024]{1,0:T(8,128)} %fusion.68, f32[2432,1024]{1,0:T(8,128)} %get-tuple-element.313, pred[]{:T(512)S(6)} %compare.3, f32[256,2432]{1,0:T(8,128)S(1)} %select_reduce_fusion.5, f32[2304,1024]{1,0:T(8,128)} %get-tuple-element.325, s32[]{:T(128)S(6)} %select_n.65), kind=kOutput, calls=%fused_computation.18.clone.1 | convolution fusion | flops 1287520256 | bytes 42860548 | tf_op jit(solution)/shard_map/while/body/eval_jaxpr/dot_general | solution.py:99
  552.1 20.1 %select_reduce_fusion.5 = f32[256,2432]{1,0:T(8,128)S(1)} fusion(f32[256,50]{0,1:T(8,128)S(1)} %dynamic-slice_convert_fusion.10, s32[256,50]{0,1:T(8,128)S(1)} %constant_dynamic-slice_fusion.5), kind=kLoop, calls=%fused_computation.14.clone.1 | loop fusion | flops 92766208 | bytes 2592768 | tf_op jit(solution)/shard_map/while/body/eval_jaxpr/reduce_sum | solution.py:17
  585.7 15.5 %fusion.69 = f32[2432,1024]{1,0:T(8,128)} fusion(f32[2432,1024]{1,0:T(8,128)} %fusion.67, f32[2432,1024]{1,0:T(8,128)} %fusion.68, f32[2432,1024]{1,0:T(8,128)} %get-tuple-element.313, pred[]{:T(512)S(6)} %compare.3, f32[256,2432]{1,0:T(8,128)S(1)} %select_reduce_fusion.5, f32[2304,1024]{1,0:T(8,128)} %get-tuple-element.325, s32[]{:T(128)S(6)} %select_n.65), kind=kOutput, calls=%fused_computation.18.clone.1 | convolution fusion | flops 1287520256 | bytes 42860548 | tf_op jit(solution)/shard_map/while/body/eval_jaxpr/dot_general | solution.py:99
  602.1 20.1 %select_reduce_fusion.5 = f32[256,2432]{1,0:T(8,128)S(1)} fusion(f32[256,50]{0,1:T(8,128)S(1)} %dynamic-slice_convert_fusion.10, s32[256,50]{0,1:T(8,128)S(1)} %constant_dynamic-slice_fusion.5), kind=kLoop, calls=%fused_computation.14.clone.1 | loop fusion | flops 92766208 | bytes 2592768 | tf_op jit(solution)/shard_map/while/body/eval_jaxpr/reduce_sum | solution.py:17
  628.7 6.9 fusion.67
  635.6 15.5 %fusion.69 = f32[2432,1024]{1,0:T(8,128)} fusion(f32[2432,1024]{1,0:T(8,128)} %fusion.67, f32[2432,1024]{1,0:T(8,128)} %fusion.68, f32[2432,1024]{1,0:T(8,128)} %get-tuple-element.313, pred[]{:T(512)S(6)} %compare.3, f32[256,2432]{1,0:T(8,128)S(1)} %select_reduce_fusion.5, f32[2304,1024]{1,0:T(8,128)} %get-tuple-element.325, s32[]{:T(128)S(6)} %select_n.65), kind=kOutput, calls=%fused_computation.18.clone.1 | convolution fusion | flops 1287520256 | bytes 42860548 | tf_op jit(solution)/shard_map/while/body/eval_jaxpr/dot_general | solution.py:99
  652.0 20.1 %select_reduce_fusion.5 = f32[256,2432]{1,0:T(8,128)S(1)} fusion(f32[256,50]{0,1:T(8,128)S(1)} %dynamic-slice_convert_fusion.10, s32[256,50]{0,1:T(8,128)S(1)} %constant_dynamic-slice_fusion.5), kind=kLoop, calls=%fused_computation.14.clone.1 | loop fusion | flops 92766208 | bytes 2592768 | tf_op jit(solution)/shard_map/while/body/eval_jaxpr/reduce_sum | solution.py:17
  685.6 15.5 %fusion.69 = f32[2432,1024]{1,0:T(8,128)} fusion(f32[2432,1024]{1,0:T(8,128)} %fusion.67, f32[2432,1024]{1,0:T(8,128)} %fusion.68, f32[2432,1024]{1,0:T(8,128)} %get-tuple-element.313, pred[]{:T(512)S(6)} %compare.3, f32[256,2432]{1,0:T(8,128)S(1)} %select_reduce_fusion.5, f32[2304,1024]{1,0:T(8,128)} %get-tuple-element.325, s32[]{:T(128)S(6)} %select_n.65), kind=kOutput, calls=%fused_computation.18.clone.1 | convolution fusion | flops 1287520256 | bytes 42860548 | tf_op jit(solution)/shard_map/while/body/eval_jaxpr/dot_general | solution.py:99
  701.9 20.1 %select_reduce_fusion.5 = f32[256,2432]{1,0:T(8,128)S(1)} fusion(f32[256,50]{0,1:T(8,128)S(1)} %dynamic-slice_convert_fusion.10, s32[256,50]{0,1:T(8,128)S(1)} %constant_dynamic-slice_fusion.5), kind=kLoop, calls=%fused_computation.14.clone.1 | loop fusion | flops 92766208 | bytes 2592768 | tf_op jit(solution)/shard_map/while/body/eval_jaxpr/reduce_sum | solution.py:17
  735.5 15.5 %fusion.69 = f32[2432,1024]{1,0:T(8,128)} fusion(f32[2432,1024]{1,0:T(8,128)} %fusion.67, f32[2432,1024]{1,0:T(8,128)} %fusion.68, f32[2432,1024]{1,0:T(8,128)} %get-tuple-element.313, pred[]{:T(512)S(6)} %compare.3, f32[256,2432]{1,0:T(8,128)S(1)} %select_reduce_fusion.5, f32[2304,1024]{1,0:T(8,128)} %get-tuple-element.325, s32[]{:T(128)S(6)} %select_n.65), kind=kOutput, calls=%fused_computation.18.clone.1 | convolution fusion | flops 1287520256 | bytes 42860548 | tf_op jit(solution)/shard_map/while/body/eval_jaxpr/dot_general | solution.py:99
  751.8 20.1 %select_reduce_fusion.5 = f32[256,2432]{1,0:T(8,128)S(1)} fusion(f32[256,50]{0,1:T(8,128)S(1)} %dynamic-slice_convert_fusion.10, s32[256,50]{0,1:T(8,128)S(1)} %constant_dynamic-slice_fusion.5), kind=kLoop, calls=%fused_computation.14.clone.1 | loop fusion | flops 92766208 | bytes 2592768 | tf_op jit(solution)/shard_map/while/body/eval_jaxpr/reduce_sum | solution.py:17
  778.5 7.0 fusion.67
  785.5 15.5 %fusion.69 = f32[2432,1024]{1,0:T(8,128)} fusion(f32[2432,1024]{1,0:T(8,128)} %fusion.67, f32[2432,1024]{1,0:T(8,128)} %fusion.68, f32[2432,1024]{1,0:T(8,128)} %get-tuple-element.313, pred[]{:T(512)S(6)} %compare.3, f32[256,2432]{1,0:T(8,128)S(1)} %select_reduce_fusion.5, f32[2304,1024]{1,0:T(8,128)} %get-tuple-element.325, s32[]{:T(128)S(6)} %select_n.65), kind=kOutput, calls=%fused_computation.18.clone.1 | convolution fusion | flops 1287520256 | bytes 42860548 | tf_op jit(solution)/shard_map/while/body/eval_jaxpr/dot_general | solution.py:99
  801.8 20.1 %select_reduce_fusion.5 = f32[256,2432]{1,0:T(8,128)S(1)} fusion(f32[256,50]{0,1:T(8,128)S(1)} %dynamic-slice_convert_fusion.10, s32[256,50]{0,1:T(8,128)S(1)} %constant_dynamic-slice_fusion.5), kind=kLoop, calls=%fused_computation.14.clone.1 | loop fusion | flops 92766208 | bytes 2592768 | tf_op jit(solution)/shard_map/while/body/eval_jaxpr/reduce_sum | solution.py:17
  828.5 6.9 fusion.67
  835.4 15.5 %fusion.69 = f32[2432,1024]{1,0:T(8,128)} fusion(f32[2432,1024]{1,0:T(8,128)} %fusion.67, f32[2432,1024]{1,0:T(8,128)} %fusion.68, f32[2432,1024]{1,0:T(8,128)} %get-tuple-element.313, pred[]{:T(512)S(6)} %compare.3, f32[256,2432]{1,0:T(8,128)S(1)} %select_reduce_fusion.5, f32[2304,1024]{1,0:T(8,128)} %get-tuple-element.325, s32[]{:T(128)S(6)} %select_n.65), kind=kOutput, calls=%fused_computation.18.clone.1 | convolution fusion | flops 1287520256 | bytes 42860548 | tf_op jit(solution)/shard_map/while/body/eval_jaxpr/dot_general | solution.py:99
  857.5 9.3 slice.14
  872.5 8.9 scatter_fusion
  881.5 10.5 convert_reduce_fusion.1
  906.3 16.8 %fusion.27 = f32[2048,1024]{1,0:T(8,128)} fusion(bf16[2304,1024]{1,0:T(8,128)(2,1)} %copy-done, bf16[2304,1024]{1,0:T(8,128)(2,1)} %bitcast.52, bf16[2304,1024]{1,0:T(8,128)(2,1)} %convert_element_type.113), kind=kOutput, calls=%fused_computation.57 | convolution fusion | flops 9682550784 | bytes 22544384 | tf_op jit(solution)/shard_map/dot_general | solution.py:76
  923.1 39.8 %all-reduce.4 = (f32[1024]{0:T(1024)S(1)}, f32[1024]{0:T(1024)S(1)}) all-reduce(f32[1024]{0:T(1024)S(1)} %get-tuple-element.215, f32[1024]{0:T(1024)S(1)} %copy-done.6), channel_id=3, replica_groups=mesh['comm'=8,'sub'=4] {'comm','sub'}, use_global_device_ids=true, to_apply=%region_12.13.clone | all-reduce | flops 2048 | bytes 16384
  964.1 11.3 slice_add_fusion
  975.4 70.6 %reduce-scatter.7.cloned.1.call-done = f32[32,1024]{1,0:T(8,128)} async-done(((f32[1024,1024]{1,0:T(8,128)}), f32[32,1024]{1,0:T(8,128)}) %reduce-scatter.7.cloned.1.call-update) | async-done | bytes 131088
  1046.0 147.7 %reduce-scatter.5.cloned.1.call-done = f32[64,1024]{1,0:T(8,128)} async-done(((f32[2048,1024]{1,0:T(8,128)}), f32[64,1024]{1,0:T(8,128)}) %reduce-scatter.5.cloned.1.call-update) | async-done | bytes 262160 | tf_op jit(solution)/shard_map/reduce_scatter | solution.py:122
  (199 shorter events, 224.8 us)
Async XLA Ops:
  7.2 54.6 %copy-start.3 = (f32[2304,50]{0,1:T(8,128)S(1)}, f32[2304,50]{0,1:T(8,128)}, u32[]{:S(2)}) copy-start(f32[2304,50]{0,1:T(8,128)} %param.21) | copy-start | bytes 1382404
  7.2 54.6 %copy-start.5 = (s32[2304]{0:T(1024)S(1)}, s32[2304]{0:T(1024)}, u32[]{:S(2)}) copy-start(s32[2304]{0:T(1024)} %param.20) | copy-start | bytes 27652
  7.2 63.5 %all-gather.3.cloned.1.call-start = ((), (), s32[]{:S(2)}) async-start(), calls=%async_computation.4 | async-start | bytes 2162688 | tf_op jit(solution)/shard_map/all_gather | solution.py:43
  8.8 339.9 %all-gather.5.cloned.1.call-start = ((), (), s32[]{:S(2)}) async-start(), calls=%async_computation.5 | async-start | bytes 4325376 | tf_op jit(solution)/shard_map/all_gather | solution.py:44
  55.0 29.0 %copy-start.7 = (f32[1024]{0:T(1024)}, f32[1024]{0:T(1024)S(1)}, u32[]{:S(2)}) copy-start(f32[1024]{0:T(1024)S(1)} %convert_element_type.117) | copy-start | bytes 12292
  61.8 30.9 %copy-start.4 = (s32[2304,50]{0,1:T(8,128)S(1)}, s32[2304,50]{0,1:T(8,128)}, u32[]{:S(2)}) copy-start(s32[2304,50]{0,1:T(8,128)} %param.19) | copy-start | bytes 1382404
  88.8 14.4 %all-to-all-start = ((bf16[32,4,1024]{2,1,0:T(4,128)(2,1)}), bf16[32,4,1024]{2,1,0:T(4,128)(2,1)S(1)}, u32[]{:S(2)}, u32[]{:S(2)}) async-start(bf16[32,4,1024]{2,1,0:T(4,128)(2,1)} %reshape.123), calls=%async_computation | async-start | bytes 524288 | tf_op jit(solution)/shard_map/all_to_all | solution.py:55
  108.5 24.4 %slice-start = ((s8[4980736]{0:T(1024)(128)(4,1)}), s8[786432]{0:T(1024)(128)(4,1)S(1)}, s32[]{:S(2)}) async-start(s8[4980736]{0:T(1024)(128)(4,1)} %bitcast.47), calls=%async_computation.8 | async-start | bytes 1572864 | tf_op jit(solution)/shard_map/while
  128.7 4.1 slice-start.1
  135.2 24.3 %slice-start = ((s8[4980736]{0:T(1024)(128)(4,1)}), s8[786432]{0:T(1024)(128)(4,1)S(1)}, s32[]{:S(2)}) async-start(s8[4980736]{0:T(1024)(128)(4,1)} %bitcast.47), calls=%async_computation.8 | async-start | bytes 1572864 | tf_op jit(solution)/shard_map/while
  155.4 4.1 slice-start.1
  161.9 24.3 %slice-start = ((s8[4980736]{0:T(1024)(128)(4,1)}), s8[786432]{0:T(1024)(128)(4,1)S(1)}, s32[]{:S(2)}) async-start(s8[4980736]{0:T(1024)(128)(4,1)} %bitcast.47), calls=%async_computation.8 | async-start | bytes 1572864 | tf_op jit(solution)/shard_map/while
  182.1 4.1 slice-start.1
  188.6 24.3 %slice-start = ((s8[4980736]{0:T(1024)(128)(4,1)}), s8[786432]{0:T(1024)(128)(4,1)S(1)}, s32[]{:S(2)}) async-start(s8[4980736]{0:T(1024)(128)(4,1)} %bitcast.47), calls=%async_computation.8 | async-start | bytes 1572864 | tf_op jit(solution)/shard_map/while
  208.8 4.1 slice-start.1
  215.3 24.3 %slice-start = ((s8[4980736]{0:T(1024)(128)(4,1)}), s8[786432]{0:T(1024)(128)(4,1)S(1)}, s32[]{:S(2)}) async-start(s8[4980736]{0:T(1024)(128)(4,1)} %bitcast.47), calls=%async_computation.8 | async-start | bytes 1572864 | tf_op jit(solution)/shard_map/while
  235.5 4.1 slice-start.1
  242.0 24.3 %slice-start = ((s8[4980736]{0:T(1024)(128)(4,1)}), s8[786432]{0:T(1024)(128)(4,1)S(1)}, s32[]{:S(2)}) async-start(s8[4980736]{0:T(1024)(128)(4,1)} %bitcast.47), calls=%async_computation.8 | async-start | bytes 1572864 | tf_op jit(solution)/shard_map/while
  262.2 4.1 slice-start.1
  268.6 24.3 %slice-start = ((s8[4980736]{0:T(1024)(128)(4,1)}), s8[786432]{0:T(1024)(128)(4,1)S(1)}, s32[]{:S(2)}) async-start(s8[4980736]{0:T(1024)(128)(4,1)} %bitcast.47), calls=%async_computation.8 | async-start | bytes 1572864 | tf_op jit(solution)/shard_map/while
  288.9 4.1 slice-start.1
  295.3 24.3 %slice-start = ((s8[4980736]{0:T(1024)(128)(4,1)}), s8[786432]{0:T(1024)(128)(4,1)S(1)}, s32[]{:S(2)}) async-start(s8[4980736]{0:T(1024)(128)(4,1)} %bitcast.47), calls=%async_computation.8 | async-start | bytes 1572864 | tf_op jit(solution)/shard_map/while
  315.6 4.1 slice-start.1
  322.0 24.3 %slice-start = ((s8[4980736]{0:T(1024)(128)(4,1)}), s8[786432]{0:T(1024)(128)(4,1)S(1)}, s32[]{:S(2)}) async-start(s8[4980736]{0:T(1024)(128)(4,1)} %bitcast.47), calls=%async_computation.8 | async-start | bytes 1572864 | tf_op jit(solution)/shard_map/while
  342.3 4.1 slice-start.1
  380.4 2.2 copy-start
  395.0 9.3 copy-start.1
  404.3 453.0 %copy-start.9 = (s32[1,32,4]{1,2,0:T(4,128)S(1)}, s32[1,32,4]{1,2,0:T(4,128)}, u32[]{:S(2)}) copy-start(s32[1,32,4]{1,2,0:T(4,128)} %param.22) | copy-start | bytes 1540
  853.0 19.3 %all-to-all-start.1 = ((f32[32,4,1024]{2,1,0:T(4,128)}), f32[32,4,1024]{2,1,0:T(4,128)S(1)}, u32[]{:S(2)}, u32[]{:S(2)}) async-start(f32[32,4,1024]{2,1,0:T(4,128)} %reshape.119), calls=%async_computation.1 | async-start | bytes 1048576 | tf_op jit(solution)/shard_map/all_to_all | solution.py:105
  856.8 189.3 %reduce-scatter.7.cloned.1.call-start = ((), (), s32[]{:S(2)}) async-start(), calls=%async_computation.7 | async-start | bytes 4325376
  866.8 14.7 %copy-start.8 = (f32[1024]{0:T(1024)S(1)}, f32[1024]{0:T(1024)}, u32[]{:S(2)}) copy-start(f32[1024]{0:T(1024)} %copy-done.7) | copy-start | bytes 12292
  872.5 21.7 %slice-start.2 = ((s8[4718592]{0:T(1024)(128)(4,1)}), s8[524288]{0:T(1024)(128)(4,1)S(1)}, s32[]{:S(2)}) async-start(s8[4718592]{0:T(1024)(128)(4,1)} %bitcast.49), calls=%async_computation.10 | async-start | bytes 1048576
  881.5 12.7 %slice-start.3 = ((s8[4718592]{0:T(1024)(128)(4,1)}), s8[4194304]{0:T(1024)(128)(4,1)S(1)}, s32[]{:S(2)}) async-start(s8[4718592]{0:T(1024)(128)(4,1)} %bitcast.49), calls=%async_computation.11 | async-start | bytes 8388608
  892.0 2.2 copy-start.2
  906.2 16.9 %copy-start.6 = (f32[1024]{0:T(1024)S(1)}, f32[1024]{0:T(1024)}, u32[]{:S(2)}) copy-start(f32[1024]{0:T(1024)} %get-tuple-element.213) | copy-start | bytes 12292
  906.2 57.9 %copy-start.10 = (bf16[1024,1024]{1,0:T(8,128)(2,1)S(1)}, bf16[1024,1024]{1,0:T(8,128)(2,1)}, u32[]{:S(2)}) copy-start(bf16[1024,1024]{1,0:T(8,128)(2,1)} %all-gather.3.cloned.1.call-done) | copy-start | bytes 6291460
  906.2 287.5 %reduce-scatter.5.cloned.1.call-start = ((), (), s32[]{:S(2)}) async-start(), calls=%async_computation.6 | async-start | bytes 8650752 | tf_op jit(solution)/shard_map/reduce_scatter | solution.py:122
Sparse Core Ops, SparseCore 0:
  11.5 59.1 all-gather.2
  74.1 61.9 all-gather.4
  906.3 139.6 reduce-scatter.6
  1048.8 144.9 reduce-scatter.4
where the time goes:
time: 1210 us; the launch traced here: 1200 us
  other arithmetic  413 us (34%)
  matrix products  394 us (33%)
  waiting for transfers between devices  243 us (20%)
  blocking collectives  81.9 us (7%)
  local copies, waits for them, and re-layouts  45.7 us (4%)
  between operations  14.2 us (1%)
    reduce_sum x18, other arithmetic, blend_parts(): jnp.sum(jnp.where(hits, alpha_block.astype(jnp.float32)[:, :, None], 0.0)...  363 us
    reduce_scatter x1, waiting for transfers between devices, shards(): lax.psum_scatter(grad_w, ('comm', 'sub'), scatter_dimension=0, tiled=True)  148 us
    dot_general x9, matrix products, spread(): lax.dot_general(lower, grad_upper, contract, preferred_element_type=jnp.f...  137 us
    unnamed x2, blocking collectives  81.9 us
    unnamed x5, waiting for transfers between devices  70.7 us
    dot_general x9, matrix products, spread(): lax.dot_general(upper, grad_lower, contract, preferred_element_type=jnp.f...  62.2 us
    dot_general x9, matrix products, spread(): lax.dot_general(upper, grad_upper, contract, preferred_element_type=jnp.f...  58.8 us
    dot_general x9, matrix products, pool_step(): jnp.dot(upper, table, preferred_element_type=jnp.float32)  36.7 us
  transfers between devices with their start and end apart: 6, of which 5 were waited for; matrix products, arithmetic and copies ran while one was open for 26% of the time, Pallas kernels for 0%

commit v1 on v0

v1 whole, which is shorter than its diff:
```python
import functools

import jax
import jax.numpy as jnp
from jax import lax
from jax.experimental import pallas as pl
from jax.experimental.pallas import tpu as pltpu
from jax.sharding import PartitionSpec as P

BF = jnp.bfloat16
F32 = jnp.float32


def finish(pre_out):
    act = jax.nn.gelu(pre_out)
    return act * lax.rsqrt(jnp.mean(act * act, axis=1, keepdims=True) + 1e-06)


def build_kernel(index_ref, count_ref, importance_ref, own_ref, halo_ref, *, rows, halo, block):
    his = (rows + halo + 255) // 256
    pairs = (his + 1) // 2
    fanout = index_ref.shape[1]
    lane = lax.broadcasted_iota(jnp.int32, (16, 128), 1)
    sublane = lax.broadcasted_iota(jnp.int32, (16, 128), 0)
    parity = (sublane >= 8).astype(jnp.int32)
    half = (lane >= 64).astype(jnp.int32)
    los = lax.broadcasted_iota(jnp.int32, (256, 128), 0).astype(BF)
    left = lax.broadcasted_iota(jnp.int32, (1, 128), 1) < 64
    hi_pattern = [(2 * t + parity).astype(BF) for t in range(pairs)]
    row_mask = [(sublane & 7) == 2 * c + half for c in range(4)]
    zero = jnp.zeros((), BF)
    one = jnp.ones((), BF)

    def twice(x):
        x = jnp.concatenate([x, jnp.zeros((16, 64 - fanout), F32)], axis=1)
        return jnp.concatenate([x, x], axis=1)

    def step(g, carry):
        at = pl.ds(pl.multiple_of(g * 16, 16), 16)
        index = index_ref[at, :]
        slot = lax.broadcasted_iota(jnp.int32, index.shape, 1)
        weight = jnp.where(slot < count_ref[at, :], importance_ref[at, :], 0.0)
        alpha = twice(weight / jnp.sum(weight, axis=1, keepdims=True))
        hi = twice((index >> 8).astype(F32))
        lo = twice((index & 255).astype(F32))
        tiles = []
        for s in range(2):
            left_parts, right_parts = [], []
            for c in range(4):
                r = s * 8 + 2 * c

                def pick(x):
                    return jnp.where(left, x[r : r + 1, :], x[r + 1 : r + 2, :]).astype(BF)

                lo_row = jnp.broadcast_to(pick(lo), (256, 128))
                right_parts.append(jnp.where(lo_row == los, one, zero))
                kept = jnp.where(row_mask[c], jnp.broadcast_to(pick(alpha), (16, 128)), zero)
                hi_row = jnp.broadcast_to(pick(hi), (16, 128))
                left_parts.append(
                    jnp.concatenate(
                        [jnp.where(hi_row == hi_pattern[t], kept, zero) for t in range(pairs)], axis=0
                    )
                )
            tiles.append(
                lax.dot_general(
                    jnp.concatenate(left_parts, axis=1),
                    jnp.concatenate(right_parts, axis=1),
                    (((1,), (1,)), ((), ())),
                    preferred_element_type=F32,
                )
            )
        for h in range(his):
            tile = jnp.concatenate([t[h * 8 : (h + 1) * 8, :] for t in tiles], axis=0).astype(BF)
            if h * 256 < rows:
                own_ref[at, h * 256 : (h + 1) * 256] = tile
            else:
                start = h * 256 - rows
                stop = min(start + 256, halo)
                halo_ref[at, start:stop] = tile[:, : stop - start]
        return carry

    lax.fori_loop(0, block // 16, step, 0, unroll=16)


def build_mixing(nbr_index, nbr_count, importance, halo):
    rows, fanout = nbr_index.shape
    block = 256
    return pl.pallas_call(
        functools.partial(build_kernel, rows=rows, halo=halo, block=block),
        grid=(rows // block,),
        in_specs=[
            pl.BlockSpec((block, fanout), lambda i: (i, 0)),
            pl.BlockSpec((block, 1), lambda i: (i, 0)),
            pl.BlockSpec((block, fanout), lambda i: (i, 0)),
        ],
        out_specs=[
            pl.BlockSpec((block, rows), lambda i: (i, 0)),
            pl.BlockSpec((block, halo), lambda i: (i, 0)),
        ],
        out_shape=[
            jax.ShapeDtypeStruct((rows, rows), BF),
            jax.ShapeDtypeStruct((rows, halo), BF),
        ],
        compiler_params=pltpu.CompilerParams(vmem_limit_bytes=40 * 2**20),
        cost_estimate=pl.CostEstimate(
            flops=2 * rows * 10 * 8 * 64 * 256, bytes_accessed=4 * rows * rows, transcendentals=0
        ),
        name="build_mixing",
    )(nbr_index, nbr_count.reshape(rows, 1), importance)


def shards(
    features,
    q_weight,
    q_bias,
    w_weight,
    w_bias,
    nbr_index,
    nbr_count,
    importance,
    send_rows,
    cotangent,
):
    devices = lax.axis_size(("comm", "sub"))
    rows, width = features.shape
    fanout = nbr_index.shape[1]
    per_peer = send_rows.shape[2]
    halo = devices * per_peer
    own_mix, halo_mix = build_mixing(nbr_index, nbr_count, importance, halo)
    q_full, w_full, qbias_full, wbias_full = (
        lax.all_gather(q_weight.astype(jnp.bfloat16), ("comm", "sub"), axis=0, tiled=True),
        lax.all_gather(w_weight.astype(jnp.bfloat16), ("comm", "sub"), axis=0, tiled=True),
        lax.all_gather(q_bias.astype(jnp.bfloat16), ("comm", "sub"), axis=0, tiled=True),
        lax.all_gather(w_bias.astype(jnp.bfloat16), ("comm", "sub"), axis=0, tiled=True),
    )
    feat_low = features.astype(jnp.bfloat16)
    pre_hidden = jnp.dot(feat_low, q_full, preferred_element_type=jnp.float32) + qbias_full.astype(
        jnp.float32
    )
    neigh_low = jax.nn.gelu(pre_hidden).astype(jnp.bfloat16)
    targets = send_rows[0]
    outgoing = neigh_low[targets]
    incoming = lax.all_to_all(outgoing, ("comm", "sub"), split_axis=0, concat_axis=0, tiled=True)
    pooled = jnp.dot(own_mix, neigh_low, preferred_element_type=F32) + jnp.dot(
        halo_mix, incoming.reshape(halo, width), preferred_element_type=F32
    )
    joined = jnp.concatenate([feat_low, pooled.astype(jnp.bfloat16)], axis=1)
    pre_out = jnp.dot(joined, w_full, preferred_element_type=jnp.float32) + wbias_full.astype(
        jnp.float32
    )
    embedding, finish_back = jax.vjp(finish, pre_out)
    grad_pre_out = finish_back(cotangent)[0].astype(jnp.bfloat16)
    grad_w = lax.dot_general(
        joined, grad_pre_out, (((0,), (0,)), ((), ())), preferred_element_type=jnp.float32
    )
    grad_wbias = jnp.sum(grad_pre_out.astype(jnp.float32), axis=0)
    grad_joined = lax.dot_general(
        grad_pre_out, w_full, (((1,), (1,)), ((), ())), preferred_element_type=jnp.float32
    )
    grad_pooled = grad_joined[:, width:]
    contract = (((0,), (0,)), ((), ()))

    grad_pooled = grad_pooled.astype(BF)
    outgoing_grad = lax.dot_general(halo_mix, grad_pooled, contract, preferred_element_type=F32)
    returned = lax.all_to_all(
        outgoing_grad.reshape(devices, per_peer, width),
        ("comm", "sub"),
        split_axis=0,
        concat_axis=0,
        tiled=True,
    )
    grad_neigh = lax.dot_general(own_mix, grad_pooled, contract, preferred_element_type=F32)
    grad_neigh = grad_neigh.at[targets.reshape(-1)].add(returned.reshape(halo, width))
    gelu_value, gelu_back = jax.vjp(jax.nn.gelu, pre_hidden)
    grad_pre_hidden = gelu_back(grad_neigh)[0].astype(jnp.bfloat16)
    grad_q = lax.dot_general(
        feat_low, grad_pre_hidden, (((0,), (0,)), ((), ())), preferred_element_type=jnp.float32
    )
    grad_qbias = jnp.sum(grad_pre_hidden.astype(jnp.float32), axis=0)
    grad_features = grad_joined[:, :width] + lax.dot_general(
        grad_pre_hidden, q_full, (((1,), (1,)), ((), ())), preferred_element_type=jnp.float32
    )
    grad_q_shard, grad_w_shard, grad_qbias_shard, grad_wbias_shard = (
        lax.psum_scatter(grad_q, ("comm", "sub"), scatter_dimension=0, tiled=True),
        lax.psum_scatter(grad_w, ("comm", "sub"), scatter_dimension=0, tiled=True),
        lax.psum_scatter(grad_qbias, ("comm", "sub"), scatter_dimension=0, tiled=True),
        lax.psum_scatter(grad_wbias, ("comm", "sub"), scatter_dimension=0, tiled=True),
    )
    return (
        embedding,
        grad_features,
        grad_q_shard,
        grad_qbias_shard,
        grad_w_shard,
        grad_wbias_shard,
    )


def solution(mesh):
    in_specs = (
        P(("comm", "sub"), None),
        P(("comm", "sub"), None),
        P(("comm", "sub")),
        P(("comm", "sub"), None),
        P(("comm", "sub")),
        P(("comm", "sub"), None),
        P(("comm", "sub")),
        P(("comm", "sub"), None),
        P(("comm", "sub"), None, None),
        P(("comm", "sub"), None),
    )
    out_specs = (
        P(("comm", "sub"), None),
        P(("comm", "sub"), None),
        P(("comm", "sub"), None),
        P(("comm", "sub")),
        P(("comm", "sub"), None),
        P(("comm", "sub")),
    )
    return jax.shard_map(shards, mesh=mesh, in_specs=in_specs, out_specs=out_specs, check_vma=False)
```

time: 1210 us -> 558 us (0.46)
  other arithmetic: 413 us -> 38 us
  matrix products: 394 us -> 127 us
  Pallas kernels: 0 us -> 29.1 us
  waiting for transfers between devices: 243 us -> 219 us
  local copies, waits for them, and re-layouts: 45.7 us -> 27.2 us
    reduce_sum x19 -> x0, other arithmetic: 363 us -> none  [the longest x18 363 us: blend_parts(): jnp.sum(jnp.where(hits, alpha_block.astype(jnp.float32)[:, :, None], 0.0)...]
    dot_general x45 -> x4, matrix products: 315 us -> 47.1 us  [the longest x1 18.1 us: shards(): lax.dot_general(own_mix, grad_pooled, contract, preferred_element_type=F32)]
    pallas_call x0 -> x1, Pallas kernels: none -> 29.1 us  [build_mixing(): pl.pallas_call(functools.partial(build_kernel, rows=rows, halo=halo, bloc...]
    slice x3 -> x0, local copies, waits for them, and re-layouts: 15.3 us -> none  [the longest x1 9.31 us: shards(): grad_table[:rows].at[targets.reshape(-1)]]
  transfers between devices with their start and end apart: 6 -> 6, of which waited for: 5 -> 2; matrix products, arithmetic and copies ran while one was open for 26% -> 19% of each run, Pallas kernels for 0% -> 5%
where the time goes in v1:
time: 558 us; the launch traced here: 550 us
  waiting for transfers between devices  219 us (39%)
  matrix products  127 us (23%)
  blocking collectives  83.5 us (15%)
  other arithmetic  38 us (7%)
  Pallas kernels  29.1 us (5%)
  local copies, waits for them, and re-layouts  27.2 us (5%)
  between operations  14.5 us (3%)
  starting transfers between devices  11.1 us (2%)
    reduce_scatter x1, waiting for transfers between devices, shards(): lax.psum_scatter(grad_w, ('comm', 'sub'), scatter_dimension=0, tiled=True)  148 us
    unnamed x2, blocking collectives  83.5 us
    unnamed x5, waiting for transfers between devices  71.7 us
    pallas_call x1, Pallas kernels, build_mixing(): pl.pallas_call(functools.partial(build_kernel, rows=rows, halo=halo, bloc...  29.1 us
    unnamed x33, local copies, waits for them, and re-layouts  19 us
    dot_general x1, matrix products, shards(): jnp.dot(joined, w_full, preferred_element_type=jnp.float32)  18.9 us
    dot_general x1, matrix products, shards(): lax.dot_general(own_mix, grad_pooled, contract, preferred_element_type=F32)  18.1 us
    dot_general x1, matrix products, shards(): jnp.dot(own_mix, neigh_low, preferred_element_type=F32)  17 us
  transfers between devices with their start and end apart: 6, of which 2 were waited for; matrix products, arithmetic and copies ran while one was open for 19% of the time, Pallas kernels for 5%

profile of v1, /device:TPU:0, one launch (start us, length us, event | category | flops | bytes accessed | tf_op | source)
XLA Modules:
  0.0 549.9 jit_solution(7652304268479172211)
XLA Ops:
  7.2 0.0 all-gather.3.cloned.1.call-start
  7.2 1.6 convert_element_type.41
  8.9 0.0 all-gather.5.cloned.1.call-start
  8.9 1.6 convert_element_type.46
  10.6 0.7 convert_element_type.42
  11.2 0.7 convert_element_type.47
  11.9 0.2 dynamic-update-slice
  12.1 0.2 dynamic-update-slice.1
  12.3 42.1 %all-reduce.5 = (bf16[1024]{0:T(1024)(128)(2,1)S(1)}, bf16[1024]{0:T(1024)(128)(2,1)S(1)}) all-reduce(bf16[1024]{0:T(1024)(128)(2,1)S(1)} %dynamic-update-slice, bf16[1024]{0:T(1024)(128)(2,1)S(1)} %dynamic-update-slice.1), channel_id=1, replica_groups=mesh['comm'=8,'sub'=4] {'comm','sub'}, use_global_device_ids=true, to_apply=%add | all-reduce | flops 2048 | bytes 8192
  54.4 7.7 %copy.31 = bf16[2304,1024]{0,1:T(8,128)(2,1)} copy(f32[2304,1024]{1,0:T(8,128)} %param.10) | data formatting | bytes 14155776 | tf_op args[0]
  62.1 0.4 copy.32.index_ref
  62.5 0.4 copy.34.importance_ref
  62.9 1.9 reshape.123.count_ref
  64.8 0.1 copy.37
  64.9 0.1 copy.35
  64.9 0.1 reshape.104
  65.1 0.1 reshape_squeeze.3
  65.2 1.3 copy-done
  66.5 29.1 %build_mixing.1 = (bf16[2304,2304]{1,0:T(8,128)(2,1)}, bf16[2304,128]{1,0:T(8,128)(2,1)S(1)}) custom-call(s32[2304,50]{1,0:T(8,128)S(1)} %copy.32.index_ref, s32[2304,1]{1,0:T(8,128)S(1)} %copy-done, f32[2304,50]{1,0:T(8,128)S(1)} %copy.34.importance_ref), custom_call_target="tpu_custom_call" | custom-call | flops 6039797760 | bytes 21233664 | tf_op jit(solution)/shard_map/build_mixing/pallas_call | solution.py:88
  95.6 13.4 %multiply_convert_fusion = (bf16[2304,1024]{1,0:T(8,128)(2,1)}, f32[2304,1024]{1,0:T(8,128)}) fusion(f32[1024]{0:T(1024)S(1)} %convert_element_type.43, bf16[2304,1024]{0,1:T(8,128)(2,1)} %copy.31, bf16[1024,1024]{1,0:T(8,128)(2,1)} %all-gather.3.cloned.1.call-done), kind=kOutput, calls=%fused_computation.29 | convolution fusion | flops 4855431168 | bytes 20975616 | tf_op jit(solution)/shard_map/dot_general | solution.py:137
  109.0 4.0 gather_fusion
  113.0 0.8 reshape.103
  113.8 5.2 all-to-all-start
  119.0 17.0 %fusion.24 = f32[2304,1024]{0,1:T(8,128)} fusion(bf16[2304,2304]{1,0:T(8,128)(2,1)} %get-tuple-element.8, bf16[2304,1024]{1,0:T(8,128)(2,1)} %get-tuple-element.41), kind=kOutput, calls=%fused_computation.46 | convolution fusion | flops 10871635968 | bytes 24772608 | tf_op jit(solution)/shard_map/dot_general | solution.py:144
  136.0 0.1 reshape.99
  136.0 7.5 %add_convert_fusion = bf16[2304,1024]{0,1:T(8,128)(2,1)} fusion(f32[2304,1024]{0,1:T(8,128)} %fusion.24, bf16[2304,128]{1,0:T(8,128)(2,1)S(1)} %get-tuple-element.9, bf16[128,1024]{1,0:T(8,128)(2,1)S(1)} %reshape.99), kind=kOutput, calls=%fused_computation.28 | convolution fusion | flops 608698368 | bytes 15007744 | tf_op jit(solution)/shard_map/dot_general | solution.py:144
  143.5 18.9 %multiply_reduce_fusion = (f32[2304]{0:T(1024)S(1)}, f32[2304]{0:T(1024)S(1)}, f32[2304,1024]{1,0:T(8,128)S(1)}) fusion(f32[2304,1024]{1,0:T(8,128)} %param.19, f32[1024]{0:T(1024)S(1)} %convert_element_type.48, bf16[2048,1024]{1,0:T(8,128)(2,1)} %all-gather.5.cloned.1.call-done, bf16[2304,1024]{0,1:T(8,128)(2,1)} %add_convert_fusion, ...), kind=kOutput, calls=%fused_computation.26 | convolution fusion | flops 9713217536 | bytes 32528384 | tf_op jit(solution)/shard_map/dot_general | solution.py:148
  162.5 13.7 %convert_reduce_fusion = (f32[1024]{0:T(1024)S(1)}, bf16[2304,1024]{1,0:T(8,128)(2,1)S(1)}, f32[2304,1024]{1,0:T(8,128)}) fusion(f32[2304]{0:T(1024)S(1)} %get-tuple-element.39, f32[2304,1024]{1,0:T(8,128)S(1)} %get-tuple-element.43, f32[1024]{0:T(1024)S(1)} %convert_element_type.48, f32[2304,1024]{1,0:T(8,128)} %param.19, f32[2304]{0:T(1024)S(1)} %get-tuple-element.40), kind=kLoop, calls=%fused_computation.24 | loop fusion | flops 68418560 | bytes 33056768 | tf_op jit(solution)/shard_map/reduce_sum | solution.py:156
  176.2 13.0 %fusion.25 = f32[2304,2048]{1,0:T(8,128)} fusion(bf16[2304,1024]{1,0:T(8,128)(2,1)S(1)} %get-tuple-element.35, bf16[2048,1024]{1,0:T(8,128)(2,1)S(1)} %copy-done.7), kind=kOutput, calls=%fused_computation.47 | convolution fusion | flops 9663676416 | bytes 27787264 | tf_op jit(solution)/shard_map/dot_general | solution.py:157
  189.2 4.5 fusion.17
  193.6 1.0 reshape.100
  194.6 5.8 %all-to-all-start.1 = ((f32[32,4,1024]{2,1,0:T(4,128)}), f32[32,4,1024]{2,1,0:T(4,128)S(1)}, u32[]{:S(2)}, u32[]{:S(2)}) async-start(f32[32,4,1024]{2,1,0:T(4,128)} %reshape.100), calls=%async_computation.1 | async-start | bytes 1048576 | tf_op jit(solution)/shard_map/all_to_all | solution.py:165
  200.4 0.0 reduce-scatter.7.cloned.1.call-start
  200.5 18.1 %fusion.16 = f32[2304,1024]{1,0:T(8,128)} fusion(bf16[2304,2304]{1,0:T(8,128)(2,1)} %get-tuple-element.8, f32[2304,2048]{1,0:T(8,128)} %fusion.25), kind=kOutput, calls=%fused_computation.35 | convolution fusion | flops 10871635968 | bytes 24772608 | tf_op jit(solution)/shard_map/dot_general | solution.py:172
  218.6 0.2 reshape.114
  218.8 9.0 %scatter_fusion = f32[2304,1024]{1,0:T(8,128)} fusion(f32[2304,1024]{1,0:T(8,128)} %fusion.16, s32[128]{0:T(128)S(1)} %fusion.19, f32[128,1024]{1,0:T(8,128)S(1)} %reshape.114), kind=kCustom, calls=%fused_computation.1 | custom fusion | flops 131072 | bytes 1573376 | tf_op jit(solution)/shard_map/scatter-add | solution.py:173
  227.8 10.7 %convert_reduce_fusion.1 = (f32[1024]{0:T(1024)S(1)}, bf16[2304,1024]{1,0:T(8,128)(2,1)S(1)}) fusion(f32[2304,1024]{1,0:T(8,128)} %scatter_fusion, f32[2304,1024]{1,0:T(8,128)} %get-tuple-element.42, f32[1024]{0:T(1024)S(1)} %convert_element_type.43), kind=kLoop, calls=%fused_computation.25 | loop fusion | flops 54262784 | bytes 23601152 | tf_op jit(solution)/shard_map/reduce_sum | solution.py:179
  238.5 2.2 copy-done.2
  240.8 6.7 %convolution_bitcast_fusion = f32[1024,1024]{0,1:T(8,128)} fusion(bf16[2304,1024]{1,0:T(8,128)(2,1)S(1)} %get-tuple-element.37, bf16[2304,1024]{0,1:T(8,128)(2,1)S(1)} %bitcast.26), kind=kOutput, calls=%fused_computation.34 | convolution fusion | flops 4831838208 | bytes 13631488 | tf_op jit(solution)/shard_map/dot_general | solution.py:176
  247.4 5.3 copy.40
  252.8 0.0 reduce-scatter.5.cloned.1.call-start
  252.8 16.7 %fusion.14 = f32[2048,1024]{1,0:T(8,128)} fusion(bf16[2304,1024]{1,0:T(8,128)(2,1)} %copy-done.1, bf16[2304,1024]{0,1:T(8,128)(2,1)} %add_convert_fusion, bf16[2304,1024]{0,1:T(8,128)(2,1)} %copy.31), kind=kOutput, calls=%fused_computation.31 | convolution fusion | flops 9682550784 | bytes 22544384 | tf_op jit(solution)/shard_map/dot_general | solution.py:153
  269.6 41.4 %all-reduce.4 = (f32[1024]{0:T(1024)S(1)}, f32[1024]{0:T(1024)S(1)}) all-reduce(f32[1024]{0:T(1024)S(1)} %get-tuple-element.36, f32[1024]{0:T(1024)S(1)} %get-tuple-element.34), channel_id=3, replica_groups=mesh['comm'=8,'sub'=4] {'comm','sub'}, use_global_device_ids=true, to_apply=%region_5.0.clone | all-reduce | flops 2048 | bytes 16384
  311.0 0.6 dynamic-slice
  311.6 0.6 dynamic-slice.1
  312.2 11.3 %slice_add_fusion = f32[2304,1024]{1,0:T(8,128)} fusion(f32[2304,2048]{1,0:T(8,128)} %fusion.25, bf16[2304,1024]{1,0:T(8,128)(2,1)} %copy-done.2, bf16[1024,1024]{1,0:T(8,128)(2,1)S(1)} %copy-done.8), kind=kOutput, calls=%fused_computation.22 | convolution fusion | flops 4834197504 | bytes 25690112 | tf_op jit(solution)/shard_map/dot_general | solution.py:180
  323.5 71.6 %reduce-scatter.7.cloned.1.call-done = f32[32,1024]{1,0:T(8,128)} async-done(((f32[1024,1024]{1,0:T(8,128)}), f32[32,1024]{1,0:T(8,128)}) %reduce-scatter.7.cloned.1.call-update) | async-done | bytes 131088
  395.2 147.7 %reduce-scatter.5.cloned.1.call-done = f32[64,1024]{1,0:T(8,128)} async-done(((f32[2048,1024]{1,0:T(8,128)}), f32[64,1024]{1,0:T(8,128)}) %reduce-scatter.5.cloned.1.call-update) | async-done | bytes 262160 | tf_op jit(solution)/shard_map/reduce_scatter | solution.py:185
  (37 shorter events, 0.2 us)
Async XLA Ops:
  7.2 54.9 %copy-start.3 = (s32[2304,50]{0,1:T(8,128)S(1)}, s32[2304,50]{0,1:T(8,128)}, u32[]{:S(2)}) copy-start(s32[2304,50]{0,1:T(8,128)} %param.15) | copy-start | bytes 1382404
  7.2 55.3 %copy-start.4 = (f32[2304,50]{0,1:T(8,128)S(1)}, f32[2304,50]{0,1:T(8,128)}, u32[]{:S(2)}) copy-start(f32[2304,50]{0,1:T(8,128)} %param.17) | copy-start | bytes 1382404
  7.2 55.7 %copy-start.5 = (s32[2304]{0:T(1024)S(1)}, s32[2304]{0:T(1024)}, u32[]{:S(2)}) copy-start(s32[2304]{0:T(1024)} %param.16) | copy-start | bytes 27652
  7.2 88.4 %all-gather.3.cloned.1.call-start = ((), (), s32[]{:S(2)}) async-start(), calls=%async_computation.4 | async-start | bytes 2162688 | tf_op jit(solution)/shard_map/all_gather | solution.py:131
  8.9 134.7 %all-gather.5.cloned.1.call-start = ((), (), s32[]{:S(2)}) async-start(), calls=%async_computation.5 | async-start | bytes 4325376 | tf_op jit(solution)/shard_map/all_gather | solution.py:132
  10.6 54.2 %copy-start.6 = (s32[1,32,4]{1,2,0:T(4,128)S(1)}, s32[1,32,4]{1,2,0:T(4,128)}, u32[]{:S(2)}) copy-start(s32[1,32,4]{1,2,0:T(4,128)} %param.18) | copy-start | bytes 1540
  65.2 1.3 copy-start
  113.8 22.2 %all-to-all-start = ((bf16[32,4,1024]{2,1,0:T(4,128)(2,1)}), bf16[32,4,1024]{2,1,0:T(4,128)(2,1)S(1)}, u32[]{:S(2)}, u32[]{:S(2)}) async-start(bf16[32,4,1024]{2,1,0:T(4,128)(2,1)} %reshape.103), calls=%async_computation | async-start | bytes 524288 | tf_op jit(solution)/shard_map/all_to_all | solution.py:143
  162.5 13.7 %copy-start.7 = (bf16[2048,1024]{1,0:T(8,128)(2,1)S(1)}, bf16[2048,1024]{1,0:T(8,128)(2,1)}, u32[]{:S(2)}) copy-start(bf16[2048,1024]{1,0:T(8,128)(2,1)} %all-gather.5.cloned.1.call-done) | copy-start | bytes 12582916
  176.2 13.0 %copy-start.1 = (bf16[2304,1024]{1,0:T(8,128)(2,1)}, bf16[2304,1024]{1,0:T(8,128)(2,1)S(1)}, u32[]{:S(2)}) copy-start(bf16[2304,1024]{1,0:T(8,128)(2,1)S(1)} %get-tuple-element.35) | copy-start | bytes 14155780
  194.6 24.0 %all-to-all-start.1 = ((f32[32,4,1024]{2,1,0:T(4,128)}), f32[32,4,1024]{2,1,0:T(4,128)S(1)}, u32[]{:S(2)}, u32[]{:S(2)}) async-start(f32[32,4,1024]{2,1,0:T(4,128)} %reshape.100), calls=%async_computation.1 | async-start | bytes 1048576 | tf_op jit(solution)/shard_map/all_to_all | solution.py:165
  200.4 194.7 %reduce-scatter.7.cloned.1.call-start = ((), (), s32[]{:S(2)}) async-start(), calls=%async_computation.7 | async-start | bytes 4325376
  218.8 21.9 %slice-start = ((s8[4718592]{0:T(1024)(128)(4,1)}), s8[524288]{0:T(1024)(128)(4,1)S(1)}, s32[]{:S(2)}) async-start(s8[4718592]{0:T(1024)(128)(4,1)} %bitcast.25), calls=%async_computation.8 | async-start | bytes 1048576
  227.8 13.0 %slice-start.1 = ((s8[4718592]{0:T(1024)(128)(4,1)}), s8[4194304]{0:T(1024)(128)(4,1)S(1)}, s32[]{:S(2)}) async-start(s8[4718592]{0:T(1024)(128)(4,1)} %bitcast.25), calls=%async_computation.9 | async-start | bytes 8388608
  238.5 2.2 copy-start.2
  252.8 59.4 %copy-start.8 = (bf16[1024,1024]{1,0:T(8,128)(2,1)S(1)}, bf16[1024,1024]{1,0:T(8,128)(2,1)}, u32[]{:S(2)}) copy-start(bf16[1024,1024]{1,0:T(8,128)(2,1)} %all-gather.3.cloned.1.call-done) | copy-start | bytes 6291460
  252.8 290.1 %reduce-scatter.5.cloned.1.call-start = ((), (), s32[]{:S(2)}) async-start(), calls=%async_computation.6 | async-start | bytes 8650752 | tf_op jit(solution)/shard_map/reduce_scatter | solution.py:185
Sparse Core Ops, SparseCore 0:
  11.5 59.2 all-gather.2
  74.2 64.0 all-gather.4
  252.9 142.2 reduce-scatter.6
  397.9 144.9 reduce-scatter.4
